TPU v7x, 256 devices: a whole 4x4x8 slice. The times are simulated.
256 devices in a mesh: batch: 256 (over x, z, y, core).
Axes of the slice: x: 4, y: 4, z: 8, core: 2. Of those that a mesh axis runs over, the one named last changes fastest.
Arguments:
- pupil_vectors: bfloat16 [196608, 768], P('batch'), may hold values from -6 to 6
- caption_vectors: bfloat16 [196608, 768], P('batch'), may hold values from -6 to 6
- mentor_unscaled_entries: bfloat16 [196608, 768], P('batch'), may hold values from -6 to 6
- mentor_group_factors: float32 [196608, 24], P('batch'), may hold values from 0.25 to 2
- partner_replica_lag: int32 [196608], P('batch'), may hold values from 0 to 2
- partner_entry_slot: int32 [196608], P('batch'), may hold values from 0 to 767
- logit_multipliers: float32 [2], replicated, may hold values from 1 to 3
- logit_shifts: float32 [2], replicated, may hold values from -2 to 0
Outputs:
- row_loss: float32 [196608], P('batch')
- student_grad: bfloat16 [196608, 768], P('batch')
- text_grad: bfloat16 [196608, 768], P('batch')
All inputs are finite; a program needn't handle non-finite values.
Results may differ from a plain program's by a relative error of at most 0.0039.
Values may be sent and summed in bfloat16 or wider, within the bound.
A program may use at most 64 MiB of HBM per device.

v0:
```python
import math

import jax
import jax.numpy as jnp
from jax import lax
from jax.sharding import PartitionSpec as P

STEPS = 2


def from_behind(value, axis, by):
    length = lax.axis_size(axis)
    return lax.ppermute(value, axis, [(i, (i + by) % length) for i in range(length)])


def dequantize(values, scales):
    group = values.shape[1] // scales.shape[1]
    wide = jnp.repeat(scales, group, axis=1)
    return (values.astype(jnp.float32) * wide).astype(jnp.bfloat16)


def signed_terms(logit, hit):
    sign = jnp.where(hit, jnp.float32(1.0), jnp.float32(-1.0))
    terms = jnp.sum(jax.nn.softplus(-sign * logit), axis=1)
    slope = (-sign * jax.nn.sigmoid(-sign * logit)).astype(jnp.bfloat16)
    return (terms, slope)


def body(
    pupil_vectors,
    caption_vectors,
    mentor_unscaled_entries,
    mentor_group_factors,
    partner_replica_lag,
    partner_entry_slot,
    logit_multipliers,
    logit_shifts,
):
    rows_here, feature_size = pupil_vectors.shape
    teacher = dequantize(mentor_unscaled_entries, mentor_group_factors)
    stacked = jnp.stack([caption_vectors, teacher])
    blocks = [stacked]
    current = stacked
    for rotation_lag in range(STEPS):
        current = from_behind(current, "batch", 1)
        blocks.append(current)
    caption_factor = logit_multipliers[0] / math.sqrt(feature_size)
    mentor_factor = logit_multipliers[1] / math.sqrt(feature_size)
    columns = jnp.arange(rows_here, dtype=jnp.int32)
    diagonal = columns[:, None] == columns[None, :]
    total = jnp.zeros((rows_here,), jnp.float32)
    grad = jnp.zeros((rows_here, feature_size), jnp.float32)
    partials = []
    for rotation_lag in range(STEPS + 1):
        caption_vector_list = blocks[rotation_lag][0]
        mentor_vector = blocks[rotation_lag][1]
        text_logit = (
            caption_factor
            * jnp.dot(pupil_vectors, caption_vector_list.T, preferred_element_type=jnp.float32)
            + logit_shifts[0]
        )
        hit = (partner_replica_lag[:, None] == rotation_lag) & (
            partner_entry_slot[:, None] == columns[None, :]
        )
        caption_penalty_parts, caption_gradient_share = signed_terms(text_logit, hit)
        teach_logit = (
            mentor_factor
            * jnp.dot(pupil_vectors, mentor_vector.T, preferred_element_type=jnp.float32)
            + logit_shifts[1]
        )
        teach_hit = diagonal & (rotation_lag == 0)
        mentor_penalty_parts, mentor_gradient_share = signed_terms(teach_logit, teach_hit)
        total = total + caption_penalty_parts + mentor_penalty_parts
        grad = grad + caption_factor * jnp.dot(
            caption_gradient_share, caption_vector_list, preferred_element_type=jnp.float32
        )
        grad = grad + mentor_factor * jnp.dot(
            mentor_gradient_share, mentor_vector, preferred_element_type=jnp.float32
        )
        partials.append(
            caption_factor
            * jnp.dot(caption_gradient_share.T, pupil_vectors, preferred_element_type=jnp.float32)
        )
    owned = partials[0] + from_behind(partials[1], "batch", -1)
    owned = owned + from_behind(partials[2], "batch", -2)
    row_loss = total / ((STEPS + 1) * rows_here)
    return (row_loss, grad.astype(jnp.bfloat16), owned.astype(jnp.bfloat16))


def solution(mesh):
    placed = (
        P("batch", None),
        P("batch", None),
        P("batch", None),
        P("batch", None),
        P("batch"),
        P("batch"),
        P(),
        P(),
    )
    return jax.shard_map(
        body,
        mesh=mesh,
        in_specs=placed,
        out_specs=(P("batch"), P("batch", None), P("batch", None)),
        check_vma=False,
    )
```

profile of v0, /device:TPU:1, one launch (start us, length us, event | category | flops | bytes accessed | tf_op | source)
XLA Modules:
  0.0 135.4 jit_solution(7600290623127117351)
XLA Ops:
  0.6 0.0 copy-start
  0.6 1.7 %copy.16 = bf16[768,768]{0,1:T(8,128)(2,1)S(1)} copy(bf16[768,768]{1,0:T(8,128)(2,1)} %param.10) | data formatting | bytes 2359296 | tf_op args[2]
  2.3 1.6 %copy.17 = bf16[768,768]{0,1:T(8,128)(2,1)S(1)} copy(bf16[768,768]{1,0:T(8,128)(2,1)} %param.9) | data formatting | bytes 2359296 | tf_op args[1]
  3.9 1.1 fusion.20
  5.0 0.0 copy-start.4
  5.0 0.0 copy-start.2
  5.0 0.2 pad_maximum_fusion
  5.3 2.8 %collective-permute-start = (bf16[2,768,768]{1,2,0:T(8,128)(2,1)S(1)}, bf16[2,768,768]{1,2,0:T(8,128)(2,1)S(1)}, u32[]{:S(2)}, u32[]{:S(2)}) collective-permute-start(bf16[2,768,768]{1,2,0:T(8,128)(2,1)S(1)} %pad_maximum_fusion), channel_id=1, source_target_pairs={{0,1},{1,2},{2,3},{3,4},{4,5},{5,6},{6,7},{7,8},{8,9},{9,10},{10,1... | collective-permute-start | bytes 7077896 | tf_op jit(solution)/shard_map/ppermute | solution.py:13
  8.0 0.6 fusion.41
  9.9 0.6 fusion.42
  10.5 2.9 %fusion.1 = (f32[768]{0:T(1024)S(1)}, f32[768,768]{0,1:T(8,128)S(1)}) fusion(f32[]{:T(128)} %bitcast.4, bf16[768,768]{0,1:T(8,128)(2,1)S(1)} %fusion.20, bf16[768,768]{1,0:T(8,128)(2,1)S(1)} %copy-done, f32[]{:T(128)} %bitcast.2), kind=kOutput, calls=%fused_computation.7 | convolution fusion | flops 913636608 | bytes 4721672 | tf_op jit(solution)/shard_map/dot_general | solution.py:68
  13.5 3.3 %fusion = (f32[768]{0:T(1024)S(1)}, f32[768,768]{0,1:T(8,128)S(1)}) fusion(f32[]{:T(128)} %bitcast.1, bf16[768,768]{1,0:T(8,128)(2,1)S(1)} %copy-done, bf16[768,768]{1,0:T(8,128)(2,1)S(1)} %copy-done.1, f32[]{:T(128)} %bitcast, s32[768]{0:T(1024)S(1)} %copy-done.5, pred[768]{0:T(1024)(128)(4,1)S(1)} %get-tuple-element.3), kind=kOutput, calls=%fused_computation.6 | convolution fusion | flops 914226432 | bytes 4725512 | tf_op jit(solution)/shard_map/dot_general | solution.py:59
  16.9 1.6 %fusion.40 = f32[768,768]{1,0:T(8,128)S(1)} fusion(bf16[768,768]{1,0:T(8,128)(2,1)S(1)} %copy-done.1, f32[768,768]{0,1:T(8,128)S(1)} %get-tuple-element.19, s32[768]{0:T(1024)S(1)} %copy-done.5, pred[768]{0:T(1024)(128)(4,1)S(1)} %get-tuple-element.3), kind=kOutput, calls=%fused_computation.80 | convolution fusion | flops 911278080 | bytes 5902080 | tf_op jit(solution)/shard_map/dot_general | solution.py:74
  18.5 15.3 %collective-permute-done = bf16[2,768,768]{1,2,0:T(8,128)(2,1)S(1)} collective-permute-done((bf16[2,768,768]{1,2,0:T(8,128)(2,1)S(1)}, bf16[2,768,768]{1,2,0:T(8,128)(2,1)S(1)}, u32[]{:S(2)}, u32[]{:S(2)}) %collective-permute-start) | collective-permute-done | bytes 2359328 | tf_op jit(solution)/shard_map/ppermute | solution.py:13
  33.8 2.5 %collective-permute-start.1 = (bf16[2,768,768]{1,2,0:T(8,128)(2,1)S(1)}, bf16[2,768,768]{1,2,0:T(8,128)(2,1)S(1)}, u32[]{:S(2)}, u32[]{:S(2)}) collective-permute-start(bf16[2,768,768]{1,2,0:T(8,128)(2,1)S(1)} %collective-permute-done), channel_id=1, source_target_pairs={{0,1},{1,2},{2,3},{3,4},{4,5},{5,6},{6,7},{7,8},{8,9},{9,10},{10,1... | collective-permute-start | bytes 7077896 | tf_op jit(solution)/shard_map/ppermute | solution.py:13
  36.3 1.6 %fusion.29 = f32[768,768]{1,0:T(8,128)S(1)} fusion(bf16[768,768]{0,1:T(8,128)(2,1)S(1)} %fusion.20, f32[768,768]{0,1:T(8,128)S(1)} %get-tuple-element.21), kind=kOutput, calls=%fused_computation.66 | convolution fusion | flops 910688256 | bytes 5898240 | tf_op jit(solution)/shard_map/dot_general | solution.py:77
  37.9 3.5 %fusion.2 = (f32[768]{0:T(1024)S(1)}, f32[768,768]{0,1:T(8,128)S(1)}) fusion(f32[]{:T(128)} %bitcast.1, bf16[768,768]{1,0:T(8,128)(2,1)S(1)} %copy-done, bf16[2,768,768]{1,2,0:T(8,128)(2,1)S(1)} %collective-permute-done, f32[]{:T(128)} %bitcast, s32[768]{0:T(1024)S(1)} %copy-done.5, pred[768]{0:T(1024)(128)(4,1)S(1)} %get-tuple-element.5), kind=kOutput, calls=%fused_computation.8 | convolution fusion | flops 914226432 | bytes 4726792 | tf_op jit(solution)/shard_map/dot_general | solution.py:59
  41.4 1.7 %convolution_multiply_fusion.1 = f32[768,768]{1,0:T(8,128)S(1)} fusion(bf16[768,768]{1,0:T(8,128)(2,1)S(1)} %copy-done, f32[]{:T(128)} %bitcast, f32[768,768]{0,1:T(8,128)S(1)} %get-tuple-element.17, s32[768]{0:T(1024)S(1)} %copy-done.5, pred[768]{0:T(1024)(128)(4,1)S(1)} %get-tuple-element.5), kind=kOutput, calls=%fused_computation.59 | convolution fusion | flops 911867904 | bytes 5902084 | tf_op jit(solution)/shard_map/dot_general | solution.py:82
  43.2 7.3 %collective-permute-start.2 = (f32[768,768]{1,0:T(8,128)S(1)}, f32[768,768]{1,0:T(8,128)S(1)}, u32[]{:S(2)}, u32[]{:S(2)}) collective-permute-start(f32[768,768]{1,0:T(8,128)S(1)} %convolution_multiply_fusion.1), channel_id=1, source_target_pairs={{0,255},{1,0},{2,1},{3,2},{4,3},{5,4},{6,5},{7,6},{8,7},{9,8},{10,... | collective-permute-start | bytes 7077896 | tf_op jit(solution)/shard_map/ppermute | solution.py:13
  50.5 2.9 %fusion.3 = (f32[768]{0:T(1024)S(1)}, f32[768,768]{1,0:T(8,128)S(1)}) fusion(f32[]{:T(128)} %bitcast.4, f32[]{:T(128)} %bitcast.2, bf16[768,768]{1,0:T(8,128)(2,1)S(1)} %copy-done, bf16[2,768,768]{1,2,0:T(8,128)(2,1)S(1)} %collective-permute-done), kind=kOutput, calls=%fused_computation.9 | convolution fusion | flops 911277312 | bytes 4721672 | tf_op jit(solution)/shard_map/dot_general | solution.py:68
  53.4 1.9 %fusion.32 = f32[768,768]{1,0:T(8,128)S(1)} fusion(bf16[2,768,768]{1,2,0:T(8,128)(2,1)S(1)} %collective-permute-done, f32[768,768]{0,1:T(8,128)S(1)} %get-tuple-element.17, s32[768]{0:T(1024)S(1)} %copy-done.5, pred[768]{0:T(1024)(128)(4,1)S(1)} %get-tuple-element.5), kind=kOutput, calls=%fused_computation.68 | convolution fusion | flops 911278080 | bytes 5903360 | tf_op jit(solution)/shard_map/dot_general | solution.py:74
  55.3 6.8 %collective-permute-done.1 = bf16[2,768,768]{1,2,0:T(8,128)(2,1)S(1)} collective-permute-done((bf16[2,768,768]{1,2,0:T(8,128)(2,1)S(1)}, bf16[2,768,768]{1,2,0:T(8,128)(2,1)S(1)}, u32[]{:S(2)}, u32[]{:S(2)}) %collective-permute-start.1) | collective-permute-done | bytes 2359328 | tf_op jit(solution)/shard_map/ppermute | solution.py:13
  62.1 3.5 %fusion.4 = (f32[768]{0:T(1024)S(1)}, f32[768,768]{0,1:T(8,128)S(1)}) fusion(f32[]{:T(128)} %bitcast.1, bf16[768,768]{1,0:T(8,128)(2,1)S(1)} %copy-done, bf16[2,768,768]{1,2,0:T(8,128)(2,1)S(1)} %collective-permute-done.1, f32[]{:T(128)} %bitcast, s32[768]{0:T(1024)S(1)} %copy-done.5, pred[768]{0:T(1024)(128)(4,1)S(1)} %get-tuple-element.4), kind=kOutput, calls=%fused_computation.10 | convolution fusion | flops 914226432 | bytes 4726792 | tf_op jit(solution)/shard_map/dot_general | solution.py:59
  65.5 1.8 %convolution_multiply_fusion = f32[768,768]{1,0:T(8,128)S(1)} fusion(bf16[768,768]{1,0:T(8,128)(2,1)S(1)} %copy-done, f32[]{:T(128)} %bitcast, f32[768,768]{0,1:T(8,128)S(1)} %get-tuple-element.13, s32[768]{0:T(1024)S(1)} %copy-done.5, pred[768]{0:T(1024)(128)(4,1)S(1)} %get-tuple-element.4), kind=kOutput, calls=%fused_computation.58 | convolution fusion | flops 911867904 | bytes 5902084 | tf_op jit(solution)/shard_map/dot_general | solution.py:82
  67.3 14.1 %collective-permute-start.3 = (f32[768,768]{1,0:T(8,128)S(1)}, f32[768,768]{1,0:T(8,128)S(1)}, u32[]{:S(2)}, u32[]{:S(2)}) collective-permute-start(f32[768,768]{1,0:T(8,128)S(1)} %convolution_multiply_fusion), channel_id=1, source_target_pairs={{0,254},{1,255},{2,0},{3,1},{4,2},{5,3},{6,4},{7,5},{8,6},{9,7},{1... | collective-permute-start | bytes 7077896 | tf_op jit(solution)/shard_map/ppermute | solution.py:13
  81.5 2.3 %fusion.30 = f32[768,768]{1,0:T(8,128)S(1)} fusion(f32[768,768]{1,0:T(8,128)S(1)} %get-tuple-element.15, f32[]{:T(128)} %bitcast.4, f32[]{:T(128)} %bitcast.2, bf16[2,768,768]{1,2,0:T(8,128)(2,1)S(1)} %collective-permute-done), kind=kOutput, calls=%fused_computation.67 | convolution fusion | flops 909508608 | bytes 5898248 | tf_op jit(solution)/shard_map/dot_general | solution.py:77
  83.7 2.9 %fusion.5 = (f32[768]{0:T(1024)S(1)}, f32[768,768]{1,0:T(8,128)S(1)}) fusion(f32[]{:T(128)} %bitcast.4, f32[]{:T(128)} %bitcast.2, bf16[768,768]{1,0:T(8,128)(2,1)S(1)} %copy-done, bf16[2,768,768]{1,2,0:T(8,128)(2,1)S(1)} %collective-permute-done.1), kind=kOutput, calls=%fused_computation.11 | convolution fusion | flops 911277312 | bytes 4721672 | tf_op jit(solution)/shard_map/dot_general | solution.py:68
  86.6 0.6 add_multiply_fusion.1
  87.2 1.9 %fusion.34 = f32[768,768]{1,0:T(8,128)S(1)} fusion(bf16[2,768,768]{1,2,0:T(8,128)(2,1)S(1)} %collective-permute-done.1, f32[768,768]{0,1:T(8,128)S(1)} %get-tuple-element.13, s32[768]{0:T(1024)S(1)} %copy-done.5, pred[768]{0:T(1024)(128)(4,1)S(1)} %get-tuple-element.4), kind=kOutput, calls=%fused_computation.70 | convolution fusion | flops 911278080 | bytes 5903360 | tf_op jit(solution)/shard_map/dot_general | solution.py:74
  89.1 3.7 %add_convert_fusion.1 = bf16[768,768]{1,0:T(8,128)(2,1)} fusion(f32[768,768]{1,0:T(8,128)S(1)} %fusion.34, f32[768,768]{1,0:T(8,128)S(1)} %fusion.30, f32[768,768]{1,0:T(8,128)S(1)} %fusion.32, f32[768,768]{1,0:T(8,128)S(1)} %fusion.29, f32[768,768]{1,0:T(8,128)S(1)} %fusion.40, f32[768,768]{1,0:T(8,128)S(1)} %get-tuple-element.11, f32[]{:T(128)} %bitcast.4, ...), kind=kOutput, calls=%fused_computation.39 | convolution fusion | flops 916586496 | bytes 16517120 | tf_op jit(solution)/shard_map/dot_general | solution.py:77
  92.8 39.8 %collective-permute-done.3 = f32[768,768]{1,0:T(8,128)S(1)} collective-permute-done((f32[768,768]{1,0:T(8,128)S(1)}, f32[768,768]{1,0:T(8,128)S(1)}, u32[]{:S(2)}, u32[]{:S(2)}) %collective-permute-start.3) | collective-permute-done | bytes 2359328 | tf_op jit(solution)/shard_map/ppermute | solution.py:13
  132.6 2.8 %add_convert_fusion = bf16[768,768]{1,0:T(8,128)(2,1)} fusion(f32[768,768]{1,0:T(8,128)S(1)} %collective-permute-done.3, f32[768,768]{1,0:T(8,128)S(1)} %collective-permute-done.2, bf16[768,768]{1,0:T(8,128)(2,1)S(1)} %copy-done, f32[]{:T(128)} %bitcast, f32[768,768]{0,1:T(8,128)S(1)} %get-tuple-element.19, s32[768]{0:T(1024)S(1)} %copy-done.5, ...), kind=kOutput, calls=%fused_computation.38 | convolution fusion | flops 913637376 | bytes 9441028 | tf_op jit(solution)/shard_map/dot_general | solution.py:82
  (11 shorter events, 0.0 us)
Async XLA Ops:
  0.6 9.9 %copy-start = (bf16[768,768]{1,0:T(8,128)(2,1)S(1)}, bf16[768,768]{1,0:T(8,128)(2,1)}, u32[]{:S(2)}) copy-start(bf16[768,768]{1,0:T(8,128)(2,1)} %param.8) | copy-start | bytes 3538948
  5.0 3.0 %copy-start.3 = (f32[2]{0:T(128)S(1)}, f32[2]{0:T(128)}, u32[]{:S(2)}) copy-start(f32[2]{0:T(128)} %param.14) | copy-start | bytes 28
  5.0 4.9 %copy-start.4 = (f32[2]{0:T(128)S(1)}, f32[2]{0:T(128)}, u32[]{:S(2)}) copy-start(f32[2]{0:T(128)} %param.15) | copy-start | bytes 28
  5.0 5.5 %copy-start.2 = (s32[768]{0:T(1024)S(1)}, s32[768]{0:T(1024)}, u32[]{:S(2)}) copy-start(s32[768]{0:T(1024)} %param.12) | copy-start | bytes 9220
  5.3 28.6 %collective-permute-start = (bf16[2,768,768]{1,2,0:T(8,128)(2,1)S(1)}, bf16[2,768,768]{1,2,0:T(8,128)(2,1)S(1)}, u32[]{:S(2)}, u32[]{:S(2)}) collective-permute-start(bf16[2,768,768]{1,2,0:T(8,128)(2,1)S(1)} %pad_maximum_fusion), channel_id=1, source_target_pairs={{0,1},{1,2},{2,3},{3,4},{4,5},{5,6},{6,7},{7,8},{8,9},{9,10},{10,1... | collective-permute-start | bytes 7077896 | tf_op jit(solution)/shard_map/ppermute | solution.py:13
  10.5 3.0 %copy-start.1 = (bf16[768,768]{1,0:T(8,128)(2,1)S(1)}, bf16[768,768]{1,0:T(8,128)(2,1)}, u32[]{:S(2)}) copy-start(bf16[768,768]{1,0:T(8,128)(2,1)} %param.9) | copy-start | bytes 3538948
  10.5 3.0 %copy-start.5 = (s32[768]{0:T(1024)S(1)}, s32[768]{0:T(1024)}, u32[]{:S(2)}) copy-start(s32[768]{0:T(1024)} %param.13) | copy-start | bytes 9220
  33.8 28.3 %collective-permute-start.1 = (bf16[2,768,768]{1,2,0:T(8,128)(2,1)S(1)}, bf16[2,768,768]{1,2,0:T(8,128)(2,1)S(1)}, u32[]{:S(2)}, u32[]{:S(2)}) collective-permute-start(bf16[2,768,768]{1,2,0:T(8,128)(2,1)S(1)} %collective-permute-done), channel_id=1, source_target_pairs={{0,1},{1,2},{2,3},{3,4},{4,5},{5,6},{6,7},{7,8},{8,9},{9,10},{10,1... | collective-permute-start | bytes 7077896 | tf_op jit(solution)/shard_map/ppermute | solution.py:13
  43.2 49.7 %collective-permute-start.2 = (f32[768,768]{1,0:T(8,128)S(1)}, f32[768,768]{1,0:T(8,128)S(1)}, u32[]{:S(2)}, u32[]{:S(2)}) collective-permute-start(f32[768,768]{1,0:T(8,128)S(1)} %convolution_multiply_fusion.1), channel_id=1, source_target_pairs={{0,255},{1,0},{2,1},{3,2},{4,3},{5,4},{6,5},{7,6},{8,7},{9,8},{10,... | collective-permute-start | bytes 7077896 | tf_op jit(solution)/shard_map/ppermute | solution.py:13
  67.3 65.3 %collective-permute-start.3 = (f32[768,768]{1,0:T(8,128)S(1)}, f32[768,768]{1,0:T(8,128)S(1)}, u32[]{:S(2)}, u32[]{:S(2)}) collective-permute-start(f32[768,768]{1,0:T(8,128)S(1)} %convolution_multiply_fusion), channel_id=1, source_target_pairs={{0,254},{1,255},{2,0},{3,1},{4,2},{5,3},{6,4},{7,5},{8,6},{9,7},{1... | collective-permute-start | bytes 7077896 | tf_op jit(solution)/shard_map/ppermute | solution.py:13
where the time goes:
time: 136 us; the launch traced here: 135 us
  waiting for transfers between devices  61.9 us (46%)
  matrix products  38.4 us (28%)
  starting transfers between devices  26.7 us (20%)
  local copies, waits for them, and re-layouts  4.44 us (3%)
  between operations  2.13 us (2%)
  other arithmetic  1.92 us (1%)
    ppermute x4, waiting for transfers between devices, from_behind(): lax.ppermute(value, axis, [(i, (i + by) % length) for i in range(length)])  61.9 us
    ppermute x4, starting transfers between devices, from_behind(): lax.ppermute(value, axis, [(i, (i + by) % length) for i in range(length)])  26.7 us
    dot_general x3, matrix products, body(): jnp.dot(pupil_vectors, caption_vector_list.T, preferred_element_type=jnp....  10.3 us
    dot_general x3, matrix products, body(): jnp.dot(pupil_vectors, mentor_vector.T, preferred_element_type=jnp.float32)  8.74 us
    dot_general x3, matrix products, body(): jnp.dot(mentor_gradient_share, mentor_vector, preferred_element_type=jnp....  7.56 us
    dot_general x3, matrix products, body(): jnp.dot(caption_gradient_share.T, pupil_vectors, preferred_element_type=j...  6.34 us
    dot_general x3, matrix products, body(): jnp.dot(caption_gradient_share, caption_vector_list, preferred_element_ty...  5.42 us
    unnamed x14, local copies, waits for them, and re-layouts  3.28 us
  transfers between devices with their start and end apart: 4, of which 3 were waited for; matrix products, arithmetic and copies ran while one was open for 28% of the time, Pallas kernels for 0%

commit v1 on v0

v1 whole, which is shorter than its diff:
```python
import math

import jax
import jax.numpy as jnp
from jax import lax
from jax.experimental import pallas as pl
from jax.experimental.pallas import tpu as pltpu
from jax.sharding import PartitionSpec as P

F32 = jnp.float32
BF16 = jnp.bfloat16
MESH = pl.DeviceIdType.MESH
LN2 = math.log(2.0)
TILE = 256


def dot(a, b, ca, cb):
    return lax.dot_general(a, b, (((ca,), (cb,)), ((), ())), preferred_element_type=F32)


def score(students, refs, factors, shifts, hits, slopes):
    count = students.shape[0]
    width = refs[0].shape[0]
    total = jnp.zeros((1, count), F32)
    for ref, factor, shift, hit_row, slope in zip(refs, factors, shifts, hits, slopes):
        product = jnp.ones((8, count), F32)
        excess = jnp.zeros((8, count), F32)
        for start in range(0, width, TILE):
            half = dot(ref[start:start + TILE, :], students, 1, 1) * factor + shift
            sign = None
            if hit_row is not None:
                rows = lax.broadcasted_iota(jnp.int32, (TILE, count), 0)
                sign = jnp.where(rows == hit_row - start, F32(-1.0), F32(1.0))
                half = half * sign
            tanh = jnp.tanh(half)
            doubled = 1.0 + tanh
            if sign is not None:
                doubled = doubled * sign
            slope[start:start + TILE, :] = doubled.astype(BF16)
            folded = (1.0 + jnp.abs(tanh)).reshape(TILE // 8, 8, count)
            positive = jnp.maximum(half, 0.0).reshape(TILE // 8, 8, count)
            for part in range(TILE // 8):
                product = product * folded[part]
                excess = excess + positive[part]
        terms = 2.0 * excess - jnp.log(product)
        total = total + (jnp.sum(terms, axis=0, keepdims=True) + F32(width * LN2))
    return total


def kernel(
    steps,
    x_hbm, t_hbm, m_hbm, scales, lag, slot, multipliers, shifts,
    loss_out, sg_hbm, tg_hbm,
    xb, text, teacher, raw, slope_t, slope_m, slope_t2, slope_m2,
    tg_own, tg_other, g_step, g_local, g_send, g_back, tg_send, tg_back, sg_stage, tg_stage,
    code_mine, code_far, loss_mine, loss_far, loss_back,
    x_ss, x_rs, g_ss, g_rs, pair_ss, pair_rs, small_ss, small_rs, load, store,
):
    rows, width = tg_own.shape
    chunk = rows // steps
    devices = lax.axis_size("batch")
    me = lax.axis_index("batch")
    core = lax.rem(me, 2)
    other = me + 1 - 2 * core
    behind = lax.rem(me + devices - 2, devices)
    ahead = lax.rem(me + 2, devices)

    barrier = pltpu.get_barrier_semaphore()
    for partner in (other, behind, ahead):
        pl.semaphore_signal(barrier, inc=1, device_id=(partner,), device_id_type=MESH)

    load_m = pltpu.make_async_copy(m_hbm, raw, load.at[0])
    load_m.start()
    load_t = pltpu.make_async_copy(t_hbm, text.at[0], load.at[1])
    load_t.start()
    load_x = [
        pltpu.make_async_copy(
            x_hbm.at[pl.ds(i * chunk, chunk)], xb.at[i, pl.ds(chunk, chunk)], load.at[2 + i]
        )
        for i in range(steps)
    ]
    for copy in load_x:
        copy.start()

    code_mine[...] = lag[...] * rows + slot[...]
    pl.semaphore_wait(barrier, 3)

    def remote(src, dst, send, recv, device):
        return pltpu.make_async_remote_copy(
            src_ref=src, dst_ref=dst, send_sem=send, recv_sem=recv,
            device_id=(device,), device_id_type=MESH,
        )

    def x_copy(i):
        return remote(
            x_hbm.at[pl.ds(i * chunk, chunk)], xb.at[i, pl.ds(0, chunk)], x_ss.at[i], x_rs.at[i], behind
        )

    def g_copy(i):
        return remote(g_send.at[i], g_back.at[i], g_ss.at[i], g_rs.at[i], ahead)

    code_copy = remote(code_mine, code_far, small_ss.at[0], small_rs.at[0], behind)
    loss_copy = remote(loss_far, loss_back, small_ss.at[1], small_rs.at[1], ahead)
    text_copy = remote(t_hbm, text.at[1], pair_ss.at[0], pair_rs.at[0], other)
    teacher_copy = remote(teacher.at[0], teacher.at[1], pair_ss.at[1], pair_rs.at[1], other)
    tg_copy = remote(tg_send, tg_back, pair_ss.at[2], pair_rs.at[2], other)

    code_copy.start()
    for i in range(steps):
        x_copy(i).start()
    text_copy.start()

    groups = scales.shape[0]
    exact = scales[...]
    high = exact.astype(BF16).astype(F32)
    middle = (exact - high).astype(BF16).astype(F32)
    low = exact - high - middle
    pieces = jnp.concatenate([high, middle, low], axis=0).astype(BF16)
    spread_rows = lax.rem(lax.broadcasted_iota(jnp.int32, (3 * groups, width), 0), groups)
    spread_cols = lax.broadcasted_iota(jnp.int32, (3 * groups, width), 1) // (width // groups)
    spread = jnp.where(spread_rows == spread_cols, F32(1.0), F32(0.0)).astype(BF16)
    load_m.wait()
    for start in range(0, rows, TILE):
        wide = dot(pieces[:, start:start + TILE], spread, 0, 0)
        teacher[0, start:start + TILE, :] = (raw[start:start + TILE, :].astype(F32) * wide).astype(BF16)
    teacher_copy.start()

    scale = F32(0.5 / math.sqrt(width))
    factor_t = multipliers[0] * scale
    factor_m = multipliers[1] * scale
    shift_t = shifts[0] * 0.5
    shift_m = shifts[1] * 0.5

    tg_own[...] = jnp.zeros_like(tg_own)
    tg_other[...] = jnp.zeros_like(tg_other)
    load_t.wait()
    for copy in load_x:
        copy.wait()
    code_copy.wait()
    text_copy.wait()
    teacher_copy.wait()

    lanes = lax.broadcasted_iota(jnp.int32, (1, chunk), 1)
    nowhere = jnp.full((1, chunk), -1, jnp.int32)

    def at_lag(code, k):
        return code - k * rows

    def step(i, carry):
        x_copy(i).wait_recv()
        far = code_far[pl.ds(i, 1), :]
        near = code_mine[pl.ds(i, 1), :]
        hit_t = jnp.concatenate([at_lag(far, 2), at_lag(near, 0)], axis=1)
        hit_m = jnp.concatenate([nowhere, lanes + i * chunk], axis=1)
        both = xb[i]
        loss = score(
            both, (text.at[0], teacher.at[0]), (factor_t, factor_m), (shift_t, shift_m),
            (hit_t, hit_m), (slope_t, slope_m),
        )
        loss_far[pl.ds(i, 1), :] = loss[:, :chunk]
        loss_mine[pl.ds(i, 1), :] = loss[:, chunk:]

        place = pl.multiple_of(core * chunk, chunk)
        picked = xb[i, pl.ds(place, chunk), :]
        on_far = (core == 0)
        code = jnp.where(on_far, far, near)
        loss2 = score(
            picked, (text.at[1], teacher.at[1]), (factor_t, factor_m), (shift_t, shift_m),
            (at_lag(code, 1), None), (slope_t2, slope_m2),
        )
        loss_far[pl.ds(i, 1), :] += jnp.where(on_far, loss2, 0.0)
        loss_mine[pl.ds(i, 1), :] += jnp.where(on_far, 0.0, loss2)

        g_step[...] = (
            dot(slope_t[...], text[0], 0, 0) * factor_t + dot(slope_m[...], teacher[0], 0, 0) * factor_m
        )
        g_step[pl.ds(place, chunk), :] += (
            dot(slope_t2[...], text[1], 0, 0) * factor_t + dot(slope_m2[...], teacher[1], 0, 0) * factor_m
        )
        g_send[i] = g_step[:chunk, :].astype(BF16)
        g_copy(i).start()
        g_local[pl.ds(i * chunk, chunk), :] = g_step[chunk:, :]
        tg_own[...] += dot(slope_t[...], both, 1, 0)
        tg_other[...] += dot(slope_t2[...], picked, 1, 0)
        return carry

    lax.fori_loop(0, steps, step, 0)

    loss_copy.start()
    tg_send[...] = tg_other[...].astype(BF16)
    tg_copy.start()

    for i in range(steps):
        at = pl.ds(i * chunk, chunk)
        g_copy(i).wait_recv()
        sg_stage[at, :] = (g_local[at, :] + g_back[i].astype(F32)).astype(BF16)
        pltpu.make_async_copy(sg_stage.at[at], sg_hbm.at[at], store.at[i]).start()
        if i == 0:
            tg_copy.wait()
            tg_stage[...] = ((tg_own[...] + tg_back[...].astype(F32)) * factor_t).astype(BF16)
            store_tg = pltpu.make_async_copy(tg_stage, tg_hbm, store.at[steps])
            store_tg.start()
    loss_copy.wait()
    loss_out[...] = (loss_mine[...] + loss_back[...]) * F32(1.0 / (3 * rows))

    for i in range(steps):
        at = pl.ds(i * chunk, chunk)
        x_copy(i).wait_send()
        g_copy(i).wait_send()
        pltpu.make_async_copy(sg_stage.at[at], sg_hbm.at[at], store.at[i]).wait()
    store_tg.wait()


def body(
    pupil_vectors,
    caption_vectors,
    mentor_unscaled_entries,
    mentor_group_factors,
    partner_replica_lag,
    partner_entry_slot,
    logit_multipliers,
    logit_shifts,
):
    rows, width = pupil_vectors.shape
    steps = 6
    chunk = rows // steps
    hbm = pl.BlockSpec(memory_space=pl.ANY)
    vmem = pl.BlockSpec(memory_space=pltpu.VMEM)
    smem = pl.BlockSpec(memory_space=pltpu.SMEM)
    full_bf16 = pltpu.VMEM((rows, width), BF16)
    full_f32 = pltpu.VMEM((rows, width), F32)
    small_f32 = pltpu.VMEM((steps, chunk), F32)
    small_i32 = pltpu.VMEM((steps, chunk), jnp.int32)
    dma = pltpu.SemaphoreType.DMA
    loss, student_grad, text_grad = pl.pallas_call(
        lambda *refs: kernel(steps, *refs),
        name="distill",
        out_shape=(
            jax.ShapeDtypeStruct((steps, chunk), F32),
            jax.ShapeDtypeStruct((rows, width), BF16),
            jax.ShapeDtypeStruct((rows, width), BF16),
        ),
        in_specs=[hbm, hbm, hbm, vmem, vmem, vmem, smem, smem],
        out_specs=(vmem, hbm, hbm),
        scratch_shapes=[
            pltpu.VMEM((steps, 2 * chunk, width), BF16),
            pltpu.VMEM((2, rows, width), BF16),
            pltpu.VMEM((2, rows, width), BF16),
            full_bf16,
            pltpu.VMEM((rows, 2 * chunk), BF16),
            pltpu.VMEM((rows, 2 * chunk), BF16),
            pltpu.VMEM((rows, chunk), BF16),
            pltpu.VMEM((rows, chunk), BF16),
            full_f32,
            full_f32,
            pltpu.VMEM((2 * chunk, width), F32),
            full_f32,
            pltpu.VMEM((steps, chunk, width), BF16),
            pltpu.VMEM((steps, chunk, width), BF16),
            full_bf16,
            full_bf16,
            full_bf16,
            full_bf16,
            small_i32, small_i32, small_f32, small_f32, small_f32,
            dma((steps,)), dma((steps,)), dma((steps,)), dma((steps,)),
            dma((3,)), dma((3,)), dma((2,)), dma((2,)),
            dma((2 + steps,)), dma((steps + 1,)),
        ],
        compiler_params=pltpu.CompilerParams(
            collective_id=0, has_side_effects=True, vmem_limit_bytes=56 * 1024 * 1024
        ),
        cost_estimate=pl.CostEstimate(
            flops=30 * rows * rows * width, bytes_accessed=12 * rows * width, transcendentals=6 * rows * rows
        ),
    )(
        pupil_vectors,
        caption_vectors,
        mentor_unscaled_entries,
        mentor_group_factors.T,
        partner_replica_lag.reshape(steps, chunk),
        partner_entry_slot.reshape(steps, chunk),
        logit_multipliers,
        logit_shifts,
    )
    return loss.reshape(rows), student_grad, text_grad


def solution(mesh):
    placed = (
        P("batch", None),
        P("batch", None),
        P("batch", None),
        P("batch", None),
        P("batch"),
        P("batch"),
        P(),
        P(),
    )
    return jax.shard_map(
        body,
        mesh=mesh,
        in_specs=placed,
        out_specs=(P("batch"), P("batch", None), P("batch", None)),
        check_vma=False,
    )
```

time: 136 us -> 59.5 us (0.44)
  waiting for transfers between devices: 61.9 us -> 0 us
  Pallas kernels: 0 us -> 54 us
  matrix products: 38.4 us -> 0 us
  starting transfers between devices: 26.7 us -> 0 us
  other arithmetic: 1.92 us -> 0 us
  between operations: 2.13 us -> 0.64 us
    ppermute x4 -> x0, waiting for transfers between devices: 61.9 us -> none  [from_behind(): lax.ppermute(value, axis, [(i, (i + by) % length) for i in range(length)])]
    pallas_call x0 -> x1, Pallas kernels: none -> 54 us  [body(): pl.pallas_call(lambda *refs: kernel(steps, *refs), name='distill', out_sh...]
    dot_general x15 -> x0, matrix products: 38.4 us -> none  [the longest x3 10.3 us: body(): jnp.dot(pupil_vectors, caption_vector_list.T, preferred_element_type=jnp....]
    ppermute x4 -> x0, starting transfers between devices: 26.7 us -> none  [from_behind(): lax.ppermute(value, axis, [(i, (i + by) % length) for i in range(length)])]
    unnamed x14 -> x5, local copies, waits for them, and re-layouts: 3.28 us -> 4.74 us
  transfers between devices with their start and end apart: 4 -> 0, of which waited for: 3 -> 0; matrix products, arithmetic and copies ran while one was open for 28% -> 0% of each run, Pallas kernels for 0% -> 0%
where the time goes in v1:
time: 59.5 us; the launch traced here: 59.4 us
  Pallas kernels  54 us (91%)
  local copies, waits for them, and re-layouts  4.74 us (8%)
  between operations  0.64 us (1%)
    pallas_call x1, Pallas kernels, body(): pl.pallas_call(lambda *refs: kernel(steps, *refs), name='distill', out_sh...  54 us
    unnamed x5, local copies, waits for them, and re-layouts  4.74 us

profile of v1, /device:TPU:1, one launch (start us, length us, event | category | flops | bytes accessed | tf_op | source)
XLA Modules:
  0.0 59.4 jit_solution(3289851957321997005)
XLA Ops:
  0.6 54.0 %distill.1 = (f32[6,128]{1,0:T(8,128)}, bf16[768,768]{1,0:T(8,128)(2,1)}, bf16[768,768]{1,0:T(8,128)(2,1)}) custom-call(bf16[768,768]{1,0:T(8,128)(2,1)} %refs_0_.1, bf16[768,768]{1,0:T(8,128)(2,1)} %refs_1_.1, bf16[768,768]{1,0:T(8,128)(2,1)} %refs_2_.1, f32[24,768]{1,0:T(8,128)} %bitcast.5, s32[6,128]{1,0:T(8,128)} %bitcast.6, s32[6,128]{1,0:T(8,128)} %bitcast.7, ...), custom_call_target="tpu_custom_call" | custom-call | flops 13589544960 | bytes 7077888 | tf_op jit(solution)/shard_map/distill/pallas_call | solution.py:235
  54.6 1.3 %copy.14 = f32[768]{0:T(1024)} copy(f32[768]{0:T(1024)} %bitcast.4) | data formatting | bytes 6144
  55.9 0.0 copy-start
  55.9 2.5 %copy.15 = bf16[768,768]{1,0:T(8,128)(2,1)} copy(bf16[768,768]{1,0:T(8,128)(2,1)} %get-tuple-element.13) | data formatting | bytes 2359296
  58.3 0.0 copy-done
  58.3 1.0 %copy.16 = bf16[768,768]{1,0:T(8,128)(2,1)} copy(bf16[768,768]{1,0:T(8,128)(2,1)S(1)} %copy-done) | data formatting | bytes 2359296
Async XLA Ops:
  55.9 2.5 %copy-start = (bf16[768,768]{1,0:T(8,128)(2,1)S(1)}, bf16[768,768]{1,0:T(8,128)(2,1)}, u32[]{:S(2)}) copy-start(bf16[768,768]{1,0:T(8,128)(2,1)} %get-tuple-element.14) | copy-start | bytes 3538948

commit v2 on v1

v2 whole, which is shorter than its diff:
```python
import math

import jax
import jax.numpy as jnp
from jax import lax
from jax.experimental import pallas as pl
from jax.experimental.pallas import tpu as pltpu
from jax.sharding import PartitionSpec as P

F32 = jnp.float32
BF16 = jnp.bfloat16
MESH = pl.DeviceIdType.MESH
LN2 = math.log(2.0)
TILE = 256
CHUNK = 128


def dot(a, b, ca, cb):
    return lax.dot_general(a, b, (((ca,), (cb,)), ((), ())), preferred_element_type=F32)


def score(students, refs, factors, shifts, hits, slopes):
    count = students.shape[0]
    width = refs[0].shape[0]
    total = jnp.zeros((1, count), F32)
    for ref, factor, shift, hit_row, slope in zip(refs, factors, shifts, hits, slopes):
        product = jnp.ones((8, count), F32)
        excess = jnp.zeros((8, count), F32)
        for start in range(0, width, TILE):
            half = dot(ref[start:start + TILE, :], students, 1, 1) * factor + shift
            sign = None
            if hit_row is not None:
                rows = lax.broadcasted_iota(jnp.int32, (TILE, count), 0)
                sign = jnp.where(rows == hit_row - start, F32(-1.0), F32(1.0))
                half = half * sign
            tanh = jnp.tanh(half)
            doubled = 1.0 + tanh
            if sign is not None:
                doubled = doubled * sign
            slope[start:start + TILE, :] = doubled.astype(BF16)
            folded = (1.0 + jnp.abs(tanh)).reshape(TILE // 8, 8, count)
            positive = jnp.maximum(half, 0.0).reshape(TILE // 8, 8, count)
            for part in range(TILE // 8):
                product = product * folded[part]
                excess = excess + positive[part]
        terms = 2.0 * excess - jnp.log(product)
        total = total + (jnp.sum(terms, axis=0, keepdims=True) + F32(width * LN2))
    return total


def kernel(
    chunk,
    x_hbm, t_hbm, m_hbm, scales_hbm, lag_hbm, slot_hbm, multipliers_hbm, shifts_hbm,
    loss_out, sg_out, tg_out,
    scales, lag, slot, multipliers, shifts,
    near, far, text, teacher, raw, near_t, near_m, far_t, part_t, far_m,
    tg_own, tg_other, g_step, g_local, g_send, g_back, tg_send, tg_back,
    code_mine, code_far, loss_mine, loss_far, loss_back,
    x_ss, x_rs, g_ss, g_rs, pair_ss, pair_rs, small_ss, small_rs, load,
):
    rows, width = tg_own.shape
    lanes = lag.shape[1]
    steps = rows // chunk
    wide_steps = rows // TILE
    devices = lax.axis_size("batch")
    me = lax.axis_index("batch")
    core = lax.rem(me, 2)
    other = me + 1 - 2 * core
    behind = lax.rem(me + devices - 2, devices)
    ahead = lax.rem(me + 2, devices)

    barrier = pltpu.get_barrier_semaphore()
    for partner in (other, behind, ahead):
        pl.semaphore_signal(barrier, inc=1, device_id=(partner,), device_id_type=MESH)

    load_m = pltpu.make_async_copy(m_hbm, raw, load.at[0])
    load_t = pltpu.make_async_copy(t_hbm, text.at[0], load.at[1])
    load_x = pltpu.make_async_copy(x_hbm, near, load.at[2])
    small = [
        pltpu.make_async_copy(source, held, load.at[3 + i])
        for i, (source, held) in enumerate((
            (lag_hbm, lag), (slot_hbm, slot), (scales_hbm, scales),
            (multipliers_hbm, multipliers), (shifts_hbm, shifts),
        ))
    ]
    for copy in small:
        copy.start()
    load_m.start()
    load_t.start()
    load_x.start()
    small[0].wait()
    small[1].wait()
    code_mine[...] = lag[...] * rows + slot[...]
    pl.semaphore_wait(barrier, 3)

    def remote(src, dst, send, recv, device):
        return pltpu.make_async_remote_copy(
            src_ref=src, dst_ref=dst, send_sem=send, recv_sem=recv,
            device_id=(device,), device_id_type=MESH,
        )

    def x_copy(i):
        at = pl.ds(i * chunk, chunk)
        return remote(x_hbm.at[at], far.at[at], x_ss.at[i], x_rs.at[i], behind)

    def g_copy(i):
        at = pl.ds(i * chunk, chunk)
        return remote(g_send.at[at], g_back.at[at], g_ss.at[i], g_rs.at[i], ahead)

    code_copy = remote(code_mine, code_far, small_ss.at[0], small_rs.at[0], behind)
    loss_copy = remote(loss_far, loss_back, small_ss.at[1], small_rs.at[1], ahead)
    text_copy = remote(t_hbm, text.at[1], pair_ss.at[0], pair_rs.at[0], other)
    teacher_copy = remote(teacher.at[0], teacher.at[1], pair_ss.at[1], pair_rs.at[1], other)
    tg_copy = remote(tg_send, tg_back, pair_ss.at[2], pair_rs.at[2], other)

    code_copy.start()
    for i in range(steps):
        x_copy(i).start()
    text_copy.start()

    for copy in small[2:]:
        copy.wait()
    groups = scales.shape[0]
    exact = scales[...]
    high = exact.astype(BF16).astype(F32)
    middle = (exact - high).astype(BF16).astype(F32)
    low = exact - high - middle
    pieces = jnp.concatenate([high, middle, low], axis=0).astype(BF16)
    spread_rows = lax.rem(lax.broadcasted_iota(jnp.int32, (3 * groups, width), 0), groups)
    spread_cols = lax.broadcasted_iota(jnp.int32, (3 * groups, width), 1) // (width // groups)
    spread = jnp.where(spread_rows == spread_cols, F32(1.0), F32(0.0)).astype(BF16)
    load_m.wait()
    for start in range(0, rows, TILE):
        wide = dot(pieces[:, start:start + TILE], spread, 0, 0)
        teacher[0, start:start + TILE, :] = (raw[start:start + TILE, :].astype(F32) * wide).astype(BF16)
    teacher_copy.start()

    scale = F32(0.5 / math.sqrt(width))
    factors = (multipliers[0] * scale, multipliers[1] * scale)
    halves = (shifts[0] * 0.5, shifts[1] * 0.5)

    def students_grad(slope_t, slope_m, k):
        return dot(slope_t[...], text[k], 0, 0) * factors[0] + dot(slope_m[...], teacher[k], 0, 0) * factors[1]

    def near_step(k, n, carry):
        at = pl.ds(pl.multiple_of(n * TILE, TILE), TILE)
        per = TILE // lanes
        code = jnp.concatenate([code_mine[pl.ds(n * per + p, 1), :] for p in range(per)], axis=1)
        diagonal = lax.broadcasted_iota(jnp.int32, (1, TILE), 1) + n * TILE if k == 0 else None
        slope_t, slope_m = near_t.at[k, :, at], near_m
        loss = score(
            near[at, :], (text.at[k], teacher.at[k]), factors, halves, (code - k * rows, diagonal),
            (slope_t, slope_m),
        )
        grad = students_grad(slope_t, slope_m, k)
        for p in range(per):
            row = pl.ds(n * per + p, 1)
            part = loss[:, p * lanes:(p + 1) * lanes]
            loss_mine[row, :] = part if k == 0 else loss_mine[row, :] + part
        g_local[at, :] = grad if k == 0 else g_local[at, :] + grad
        return carry

    load_t.wait()
    load_x.wait()
    lax.fori_loop(0, wide_steps, lambda n, carry: near_step(0, n, carry), 0)
    code_copy.wait()
    text_copy.wait()
    teacher_copy.wait()

    per = lanes // chunk

    def far_job(k, i, part, code):
        at = pl.ds(pl.multiple_of(i * chunk, chunk), chunk)
        slope_t, slope_m = part_t.at[part, k], far_m
        loss = score(
            far[at, :], (text.at[k], teacher.at[k]), factors, halves, (code - (2 - k) * rows, None),
            (slope_t, slope_m),
        )
        grad = students_grad(slope_t, slope_m, k)
        place = (pl.ds(i // per, 1), pl.ds(part * chunk, chunk))
        loss_far[place] = loss if k == 0 else loss_far[place] + loss
        g_step[...] = grad if k == 0 else g_step[...] + grad

    def keep_slopes(k, outer):
        columns = pl.ds(pl.multiple_of(outer * lanes, lanes), lanes)
        far_t[k, :, columns] = jnp.concatenate([part_t[part, k] for part in range(per)], axis=1)

    def far_step(outer, carry):
        for part in range(per):
            i = outer * per + part
            x_copy(i).wait_recv()
            code = code_far[pl.ds(outer, 1), pl.ds(part * chunk, chunk)]
            far_job(0, i, part, code)

            @pl.when(core == 0)
            def _():
                far_job(1, i, part, code)

            g_send[pl.ds(pl.multiple_of(i * chunk, chunk), chunk), :] = g_step[...].astype(BF16)
            g_copy(i).start()
        keep_slopes(0, outer)

        @pl.when(core == 0)
        def _():
            keep_slopes(1, outer)

        @pl.when(jnp.logical_and(core == 1, lax.rem(outer, 2) == 0))
        def _():
            near_step(1, outer // 2, 0)
        return carry

    lax.fori_loop(0, rows // lanes, far_step, 0)
    loss_copy.start()

    @pl.when(core == 0)
    def _():
        tg_other[...] = dot(far_t[1], far[...], 1, 0)

    @pl.when(core == 1)
    def _():
        tg_other[...] = dot(near_t[1], near[...], 1, 0)

    tg_send[...] = tg_other[...].astype(BF16)
    tg_copy.start()
    tg_own[...] = dot(near_t[0], near[...], 1, 0)
    tg_own[...] += dot(far_t[0], far[...], 1, 0)

    for i in range(steps):
        at = pl.ds(i * chunk, chunk)
        g_copy(i).wait_recv()
        sg_out[at, :] = (g_local[at, :] + g_back[at, :].astype(F32)).astype(BF16)
        if i == steps // 2:
            tg_copy.wait()
            tg_out[...] = ((tg_own[...] + tg_back[...].astype(F32)) * factors[0]).astype(BF16)
    loss_copy.wait()
    loss_out[...] = (loss_mine[...] + loss_back[...]) * F32(1.0 / (3 * rows))
    for i in range(steps):
        x_copy(i).wait_send()
        g_copy(i).wait_send()


def write_out(*refs):
    count = len(refs) // 2
    done = refs[-1]
    copies = [pltpu.make_async_copy(refs[i], refs[count + i], done.at[i]) for i in range(count)]
    for copy in copies:
        copy.start()
    for copy in copies:
        copy.wait()


def body(
    pupil_vectors,
    caption_vectors,
    mentor_unscaled_entries,
    mentor_group_factors,
    partner_replica_lag,
    partner_entry_slot,
    logit_multipliers,
    logit_shifts,
):
    rows, width = pupil_vectors.shape
    chunk = CHUNK
    steps = rows // chunk
    lanes = 128
    hbm = pl.BlockSpec(memory_space=pl.ANY)
    vmem = pl.BlockSpec(memory_space=pltpu.VMEM)
    full_bf16 = pltpu.VMEM((rows, width), BF16)
    full_f32 = pltpu.VMEM((rows, width), F32)
    small_f32 = pltpu.VMEM((rows // lanes, lanes), F32)
    small_i32 = pltpu.VMEM((rows // lanes, lanes), jnp.int32)
    dma = pltpu.SemaphoreType.DMA
    results = pl.pallas_call(
        lambda *refs: kernel(chunk, *refs),
        name="distill",
        out_shape=(
            pltpu.VMEM((rows // lanes, lanes), F32),
            pltpu.VMEM((rows, width), BF16),
            pltpu.VMEM((rows, width), BF16),
        ),
        in_specs=[hbm] * 8,
        out_specs=(vmem, vmem, vmem),
        scratch_shapes=[
            pltpu.VMEM(mentor_group_factors.shape[::-1], F32),
            small_i32,
            small_i32,
            pltpu.SMEM(logit_multipliers.shape, F32),
            pltpu.SMEM(logit_shifts.shape, F32),
            full_bf16,
            full_bf16,
            pltpu.VMEM((2, rows, width), BF16),
            pltpu.VMEM((2, rows, width), BF16),
            full_bf16,
            pltpu.VMEM((2, rows, rows), BF16),
            pltpu.VMEM((rows, TILE), BF16),
            pltpu.VMEM((2, rows, rows), BF16),
            pltpu.VMEM((lanes // chunk, 2, rows, chunk), BF16),
            pltpu.VMEM((rows, chunk), BF16),
            full_f32,
            full_f32,
            pltpu.VMEM((chunk, width), F32),
            full_f32,
            full_bf16,
            full_bf16,
            full_bf16,
            full_bf16,
            small_i32, small_i32, small_f32, small_f32, small_f32,
            dma((steps,)), dma((steps,)), dma((steps,)), dma((steps,)),
            dma((3,)), dma((3,)), dma((2,)), dma((2,)),
            dma((8,)),
        ],
        compiler_params=pltpu.CompilerParams(
            collective_id=0, has_side_effects=True, vmem_limit_bytes=56 * 1024 * 1024
        ),
        cost_estimate=pl.CostEstimate(
            flops=30 * rows * rows * width, bytes_accessed=12 * rows * width, transcendentals=6 * rows * rows
        ),
    )(
        pupil_vectors,
        caption_vectors,
        mentor_unscaled_entries,
        mentor_group_factors.T,
        partner_replica_lag.reshape(rows // lanes, lanes),
        partner_entry_slot.reshape(rows // lanes, lanes),
        logit_multipliers,
        logit_shifts,
    )
    loss, student_grad, text_grad = pl.pallas_call(
        write_out,
        name="write_out",
        out_shape=(
            jax.ShapeDtypeStruct((rows // lanes, lanes), F32),
            jax.ShapeDtypeStruct((rows, width), BF16),
            jax.ShapeDtypeStruct((rows, width), BF16),
        ),
        in_specs=[vmem, vmem, vmem],
        out_specs=(hbm, hbm, hbm),
        scratch_shapes=[dma((3,))],
    )(*(pltpu.with_memory_space_constraint(result, pltpu.VMEM) for result in results))
    return loss.reshape(rows), student_grad, text_grad


def solution(mesh):
    placed = (
        P("batch", None),
        P("batch", None),
        P("batch", None),
        P("batch", None),
        P("batch"),
        P("batch"),
        P(),
        P(),
    )
    return jax.shard_map(
        body,
        mesh=mesh,
        in_specs=placed,
        out_specs=(P("batch"), P("batch", None), P("batch", None)),
        check_vma=False,
    )
```

time: 59.5 us -> 53.1 us (0.89)
  local copies, waits for them, and re-layouts: 4.74 us -> 0 us
  Pallas kernels: 54 us -> 52.3 us
    unnamed x5 -> x0, local copies, waits for them, and re-layouts: 4.74 us -> none
    pallas_call x1 -> x2, Pallas kernels: 54 us -> 52.3 us  [the longest x1 50.9 us: body(): pl.pallas_call(lambda *refs: kernel(chunk, *refs), name='distill', out_sh...]
where the time goes in v2:
time: 53.1 us; the launch traced here: 53 us
  Pallas kernels  52.3 us (98%)
  between operations  0.64 us (1%)
    pallas_call x1, Pallas kernels, body(): pl.pallas_call(lambda *refs: kernel(chunk, *refs), name='distill', out_sh...  50.9 us
    pallas_call x1, Pallas kernels, body(): pl.pallas_call(write_out, name='write_out', out_shape=(jax.ShapeDtypeStru...  1.43 us

profile of v2, /device:TPU:1, one launch (start us, length us, event | category | flops | bytes accessed | tf_op | source)
XLA Modules:
  0.0 53.0 jit_solution(12265096945691915497)
XLA Ops:
  0.6 50.9 %distill.1 = (f32[6,128]{1,0:T(8,128)S(1)}, bf16[768,768]{1,0:T(8,128)(2,1)S(1)}, bf16[768,768]{1,0:T(8,128)(2,1)S(1)}) custom-call(bf16[768,768]{1,0:T(8,128)(2,1)} %refs_0_.1, bf16[768,768]{1,0:T(8,128)(2,1)} %refs_1_.1, bf16[768,768]{1,0:T(8,128)(2,1)} %refs_2_.1, f32[24,768]{1,0:T(8,128)} %bitcast.4, s32[6,128]{1,0:T(8,128)} %bitcast.5, ...), custom_call_target="tpu_custom_call" | custom-call | flops 13589544960 | bytes 7077888 | tf_op jit(solution)/shard_map/distill/pallas_call | solution.py:273
  51.5 1.4 %write_out.1 = (f32[6,128]{1,0:T(8,128)}, bf16[768,768]{1,0:T(8,128)(2,1)}, bf16[768,768]{1,0:T(8,128)(2,1)}) custom-call(f32[6,128]{1,0:T(8,128)S(1)} %get-tuple-element.9.refs_0_, bf16[768,768]{1,0:T(8,128)(2,1)S(1)} %get-tuple-element.10.refs_1_, bf16[768,768]{1,0:T(8,128)(2,1)S(1)} %get-tuple-element.11.refs_2_), custom_call_target="tpu_custom_call" | custom-call | tf_op jit(solution)/shard_map/write_out/pallas_call | solution.py:328

commit v3 on v2

--- a/solution.py
+++ b/solution.py
@@ -12,7 +12,7 @@
 MESH = pl.DeviceIdType.MESH
 LN2 = math.log(2.0)
 TILE = 256
-CHUNK = 128
+CHUNK = 96
 
 
 def dot(a, b, ca, cb):
@@ -48,14 +48,25 @@
     return total
 
 
+def regroup(source, target):
+    long, short = source.shape[1], target.shape[1]
+    for row in range(target.shape[0]):
+        done = 0
+        while done < short:
+            line, column = divmod(row * short + done, long)
+            count = min(short - done, long - column)
+            target[row:row + 1, done:done + count] = source[line:line + 1, column:column + count]
+            done += count
+
+
 def kernel(
     chunk,
     x_hbm, t_hbm, m_hbm, scales_hbm, lag_hbm, slot_hbm, multipliers_hbm, shifts_hbm,
     loss_out, sg_out, tg_out,
     scales, lag, slot, multipliers, shifts,
-    near, far, text, teacher, raw, near_t, near_m, far_t, part_t, far_m,
-    tg_own, tg_other, g_step, g_local, g_send, g_back, tg_send, tg_back,
-    code_mine, code_far, loss_mine, loss_far, loss_back,
+    near, far, text, teacher, raw, near_t, near_m, far_t, far_m,
+    tg_own, tg_other, g_local, g_send, g_back, tg_send, tg_back,
+    code_mine, code_send, code_far, loss_mine, loss_far, loss_back, loss_wide,
     x_ss, x_rs, g_ss, g_rs, pair_ss, pair_rs, small_ss, small_rs, load,
 ):
     rows, width = tg_own.shape
@@ -91,6 +102,7 @@
     small[0].wait()
     small[1].wait()
     code_mine[...] = lag[...] * rows + slot[...]
+    regroup(code_mine, code_send)
     pl.semaphore_wait(barrier, 3)
 
     def remote(src, dst, send, recv, device):
@@ -107,7 +119,7 @@
         at = pl.ds(i * chunk, chunk)
         return remote(g_send.at[at], g_back.at[at], g_ss.at[i], g_rs.at[i], ahead)
 
-    code_copy = remote(code_mine, code_far, small_ss.at[0], small_rs.at[0], behind)
+    code_copy = remote(code_send, code_far, small_ss.at[0], small_rs.at[0], behind)
     loss_copy = remote(loss_far, loss_back, small_ss.at[1], small_rs.at[1], ahead)
     text_copy = remote(t_hbm, text.at[1], pair_ss.at[0], pair_rs.at[0], other)
     teacher_copy = remote(teacher.at[0], teacher.at[1], pair_ss.at[1], pair_rs.at[1], other)
@@ -167,54 +179,50 @@
     text_copy.wait()
     teacher_copy.wait()
 
-    per = lanes // chunk
-
-    def far_job(k, i, part, code):
+    def far_job(blocks, i):
         at = pl.ds(pl.multiple_of(i * chunk, chunk), chunk)
-        slope_t, slope_m = part_t.at[part, k], far_m
-        loss = score(
-            far[at, :], (text.at[k], teacher.at[k]), factors, halves, (code - (2 - k) * rows, None),
-            (slope_t, slope_m),
-        )
-        grad = students_grad(slope_t, slope_m, k)
-        place = (pl.ds(i // per, 1), pl.ds(part * chunk, chunk))
-        loss_far[place] = loss if k == 0 else loss_far[place] + loss
-        g_step[...] = grad if k == 0 else g_step[...] + grad
-
-    def keep_slopes(k, outer):
-        columns = pl.ds(pl.multiple_of(outer * lanes, lanes), lanes)
-        far_t[k, :, columns] = jnp.concatenate([part_t[part, k] for part in range(per)], axis=1)
-
-    def far_step(outer, carry):
-        for part in range(per):
-            i = outer * per + part
-            x_copy(i).wait_recv()
-            code = code_far[pl.ds(outer, 1), pl.ds(part * chunk, chunk)]
-            far_job(0, i, part, code)
-
-            @pl.when(core == 0)
-            def _():
-                far_job(1, i, part, code)
-
-            g_send[pl.ds(pl.multiple_of(i * chunk, chunk), chunk), :] = g_step[...].astype(BF16)
-            g_copy(i).start()
-        keep_slopes(0, outer)
+        row = pl.ds(i, 1)
+        code = code_far[row, :]
+        refs, hits, slopes = [], [], []
+        for k in range(blocks):
+            refs += [text.at[k], teacher.at[k]]
+            hits += [code - (2 - k) * rows, None]
+            slopes += [far_t.at[i, k], far_m.at[k]]
+        loss_far[row, :] = score(far[at, :], refs, factors * blocks, halves * blocks, hits, slopes)
+        grads = [
+            sum(dot(slopes[2 * k + side][...], refs[2 * k + side][...], 0, 0) for k in range(blocks))
+            for side in range(2)
+        ]
+        g_send[at, :] = (grads[0] * factors[0] + grads[1] * factors[1]).astype(BF16)
+
+    def far_step(i, carry):
+        x_copy(i).wait_recv()
 
         @pl.when(core == 0)
         def _():
-            keep_slopes(1, outer)
-
-        @pl.when(jnp.logical_and(core == 1, lax.rem(outer, 2) == 0))
+            far_job(2, i)
+
+        @pl.when(core == 1)
         def _():
-            near_step(1, outer // 2, 0)
+            far_job(1, i)
+
+        g_copy(i).start()
+
+        @pl.when((core == 1) & (lax.rem(i, 2) == 0) & (i < 2 * wide_steps))
+        def _():
+            near_step(1, i // 2, 0)
         return carry
 
-    lax.fori_loop(0, rows // lanes, far_step, 0)
+    def far_text_grad(k):
+        slopes = jnp.concatenate([far_t[i, k] for i in range(steps)], axis=1)
+        return dot(slopes, far[...], 1, 0)
+
+    lax.fori_loop(0, steps, far_step, 0)
     loss_copy.start()
 
     @pl.when(core == 0)
     def _():
-        tg_other[...] = dot(far_t[1], far[...], 1, 0)
+        tg_other[...] = far_text_grad(1)
 
     @pl.when(core == 1)
     def _():
@@ -223,7 +231,7 @@
     tg_send[...] = tg_other[...].astype(BF16)
     tg_copy.start()
     tg_own[...] = dot(near_t[0], near[...], 1, 0)
-    tg_own[...] += dot(far_t[0], far[...], 1, 0)
+    tg_own[...] += far_text_grad(0)
 
     for i in range(steps):
         at = pl.ds(i * chunk, chunk)
@@ -233,7 +241,8 @@
             tg_copy.wait()
             tg_out[...] = ((tg_own[...] + tg_back[...].astype(F32)) * factors[0]).astype(BF16)
     loss_copy.wait()
-    loss_out[...] = (loss_mine[...] + loss_back[...]) * F32(1.0 / (3 * rows))
+    regroup(loss_back, loss_wide)
+    loss_out[...] = (loss_mine[...] + loss_wide[...]) * F32(1.0 / (3 * rows))
     for i in range(steps):
         x_copy(i).wait_send()
         g_copy(i).wait_send()
@@ -293,18 +302,22 @@
             full_bf16,
             pltpu.VMEM((2, rows, rows), BF16),
             pltpu.VMEM((rows, TILE), BF16),
-            pltpu.VMEM((2, rows, rows), BF16),
-            pltpu.VMEM((lanes // chunk, 2, rows, chunk), BF16),
-            pltpu.VMEM((rows, chunk), BF16),
+            pltpu.VMEM((steps, 2, rows, chunk), BF16),
+            pltpu.VMEM((2, rows, chunk), BF16),
             full_f32,
             full_f32,
-            pltpu.VMEM((chunk, width), F32),
             full_f32,
             full_bf16,
             full_bf16,
             full_bf16,
             full_bf16,
-            small_i32, small_i32, small_f32, small_f32, small_f32,
+            small_i32,
+            pltpu.VMEM((steps, chunk), jnp.int32),
+            pltpu.VMEM((steps, chunk), jnp.int32),
+            small_f32,
+            pltpu.VMEM((steps, chunk), F32),
+            pltpu.VMEM((steps, chunk), F32),
+            small_f32,
             dma((steps,)), dma((steps,)), dma((steps,)), dma((steps,)),
             dma((3,)), dma((3,)), dma((2,)), dma((2,)),
             dma((8,)),

time: 53.1 us -> 51.7 us (0.974)
  Pallas kernels: 52.3 us -> 51 us
    pallas_call x1, Pallas kernels: 50.9 us -> 49.5 us  [body(): pl.pallas_call(lambda *refs: kernel(chunk, *refs), name='distill', out_sh...]
where the time goes in v3:
time: 51.7 us; the launch traced here: 51.6 us
  Pallas kernels  51 us (99%)
  between operations  0.64 us (1%)
    pallas_call x1, Pallas kernels, body(): pl.pallas_call(lambda *refs: kernel(chunk, *refs), name='distill', out_sh...  49.5 us
    pallas_call x1, Pallas kernels, body(): pl.pallas_call(write_out, name='write_out', out_shape=(jax.ShapeDtypeStru...  1.43 us

profile of v3, /device:TPU:1, one launch (start us, length us, event | category | flops | bytes accessed | tf_op | source)
XLA Modules:
  0.0 51.6 jit_solution(14643348944404511813)
XLA Ops:
  0.6 49.5 %distill.1 = (f32[6,128]{1,0:T(8,128)S(1)}, bf16[768,768]{1,0:T(8,128)(2,1)S(1)}, bf16[768,768]{1,0:T(8,128)(2,1)S(1)}) custom-call(bf16[768,768]{1,0:T(8,128)(2,1)} %refs_0_.1, bf16[768,768]{1,0:T(8,128)(2,1)} %refs_1_.1, bf16[768,768]{1,0:T(8,128)(2,1)} %refs_2_.1, f32[24,768]{1,0:T(8,128)} %bitcast.4, s32[6,128]{1,0:T(8,128)} %bitcast.5, ...), custom_call_target="tpu_custom_call" | custom-call | flops 13589544960 | bytes 7077888 | tf_op jit(solution)/shard_map/distill/pallas_call | solution.py:282
  50.2 1.4 %write_out.1 = (f32[6,128]{1,0:T(8,128)}, bf16[768,768]{1,0:T(8,128)(2,1)}, bf16[768,768]{1,0:T(8,128)(2,1)}) custom-call(f32[6,128]{1,0:T(8,128)S(1)} %get-tuple-element.9.refs_0_, bf16[768,768]{1,0:T(8,128)(2,1)S(1)} %get-tuple-element.10.refs_1_, bf16[768,768]{1,0:T(8,128)(2,1)S(1)} %get-tuple-element.11.refs_2_), custom_call_target="tpu_custom_call" | custom-call | tf_op jit(solution)/shard_map/write_out/pallas_call | solution.py:341

commit v4 on v3

--- a/solution.py
+++ b/solution.py
@@ -13,6 +13,9 @@
 LN2 = math.log(2.0)
 TILE = 256
 CHUNK = 96
+GRID = (4, 8, 4)
+X_RELAYED, X_FORWARD = 4, 3
+G_RELAYED, G_FORWARD = 4, 7
 
 
 def dot(a, b, ca, cb):
@@ -68,6 +71,7 @@
     tg_own, tg_other, g_local, g_send, g_back, tg_send, tg_back,
     code_mine, code_send, code_far, loss_mine, loss_far, loss_back, loss_wide,
     x_ss, x_rs, g_ss, g_rs, pair_ss, pair_rs, small_ss, small_rs, load,
+    x_hold, g_hold, relay_ss, relay_rs, entered,
 ):
     rows, width = tg_own.shape
     lanes = lag.shape[1]
@@ -80,9 +84,45 @@
     behind = lax.rem(me + devices - 2, devices)
     ahead = lax.rem(me + 2, devices)
 
+    nx, nz, ny = GRID
+    x_at, z_at, y_at = me // (nz * ny * 2), lax.rem(me // (ny * 2), nz), lax.rem(me // 2, ny)
+
+    def device(x, z, y):
+        return ((lax.rem(x + nx, nx) * nz + z) * ny + y) * 2 + core
+
+    is_source = (z_at == 0) & (y_at == 0)
+    is_target = (z_at == nz - 1) & (y_at == ny - 1)
+    is_x_relay = (z_at == 0) & (y_at == ny - 1)
+    is_g_relay = (z_at == nz - 1) & (y_at == 0)
+    source = device(x_at + 1, 0, 0)
+    target = device(x_at, nz - 1, ny - 1)
+    source_x_relay = device(x_at - 1, 0, ny - 1)
+    target_x_relay = device(x_at, 0, ny - 1)
+    target_g_relay = device(x_at + 1, nz - 1, 0)
+    source_g_relay = device(x_at, nz - 1, 0)
+    g_relay_source = device(x_at, 0, 0)
+    g_relay_target = device(x_at - 1, nz - 1, ny - 1)
+
     barrier = pltpu.get_barrier_semaphore()
+
+    def greet(partner):
+        pl.semaphore_signal(barrier, inc=1, device_id=(partner,), device_id_type=MESH)
+
     for partner in (other, behind, ahead):
-        pl.semaphore_signal(barrier, inc=1, device_id=(partner,), device_id_type=MESH)
+        greet(partner)
+
+    @pl.when(is_source)
+    def _():
+        greet(source_g_relay)
+
+    @pl.when(is_x_relay)
+    def _():
+        greet(source)
+        greet(target)
+
+    @pl.when(is_g_relay)
+    def _():
+        greet(g_relay_target)
 
     load_m = pltpu.make_async_copy(m_hbm, raw, load.at[0])
     load_t = pltpu.make_async_copy(t_hbm, text.at[0], load.at[1])
@@ -103,7 +143,11 @@
     small[1].wait()
     code_mine[...] = lag[...] * rows + slot[...]
     regroup(code_mine, code_send)
-    pl.semaphore_wait(barrier, 3)
+    pl.semaphore_wait(barrier, 3 + jnp.where(is_target, 2, jnp.where(is_source | is_g_relay, 1, 0)))
+
+    @pl.when(is_target)
+    def _():
+        pl.semaphore_signal(entered, inc=1, device_id=(target_x_relay,), device_id_type=MESH)
 
     def remote(src, dst, send, recv, device):
         return pltpu.make_async_remote_copy(
@@ -119,6 +163,17 @@
         at = pl.ds(i * chunk, chunk)
         return remote(g_send.at[at], g_back.at[at], g_ss.at[i], g_rs.at[i], ahead)
 
+    step_x = pl.ds(X_RELAYED * chunk, chunk)
+    step_g = pl.ds(G_RELAYED * chunk, chunk)
+    x_to_relay = remote(
+        x_hbm.at[step_x], x_hold, x_ss.at[X_RELAYED], relay_rs.at[0], source_x_relay
+    )
+    x_from_relay = remote(x_hold, far.at[step_x], relay_ss.at[0], x_rs.at[X_RELAYED], target)
+    g_to_relay = remote(
+        g_send.at[step_g], g_hold, g_ss.at[G_RELAYED], relay_rs.at[1], target_g_relay
+    )
+    g_from_relay = remote(g_hold, g_back.at[step_g], relay_ss.at[1], g_rs.at[G_RELAYED], g_relay_source)
+
     code_copy = remote(code_send, code_far, small_ss.at[0], small_rs.at[0], behind)
     loss_copy = remote(loss_far, loss_back, small_ss.at[1], small_rs.at[1], ahead)
     text_copy = remote(t_hbm, text.at[1], pair_ss.at[0], pair_rs.at[0], other)
@@ -126,8 +181,16 @@
     tg_copy = remote(tg_send, tg_back, pair_ss.at[2], pair_rs.at[2], other)
 
     code_copy.start()
+
+    @pl.when(is_source)
+    def _():
+        x_to_relay.start()
+
     for i in range(steps):
-        x_copy(i).start()
+        if i == X_RELAYED:
+            pl.when(jnp.logical_not(is_source))(x_copy(i).start)
+        else:
+            x_copy(i).start()
     text_copy.start()
 
     for copy in small[2:]:
@@ -206,7 +269,24 @@
         def _():
             far_job(1, i)
 
-        g_copy(i).start()
+        @pl.when(is_target & (i == G_RELAYED))
+        def _():
+            g_to_relay.start()
+
+        @pl.when(jnp.logical_not(is_target & (i == G_RELAYED)))
+        def _():
+            g_copy(i).start()
+
+        @pl.when(is_x_relay & (i == X_FORWARD))
+        def _():
+            pl.semaphore_wait(entered, 1)
+            x_to_relay.wait_recv()
+            x_from_relay.start()
+
+        @pl.when(is_g_relay & (i == G_FORWARD))
+        def _():
+            g_to_relay.wait_recv()
+            g_from_relay.start()
 
         @pl.when((core == 1) & (lax.rem(i, 2) == 0) & (i < 2 * wide_steps))
         def _():
@@ -246,6 +326,14 @@
     for i in range(steps):
         x_copy(i).wait_send()
         g_copy(i).wait_send()
+
+    @pl.when(is_x_relay)
+    def _():
+        x_from_relay.wait_send()
+
+    @pl.when(is_g_relay)
+    def _():
+        g_from_relay.wait_send()
 
 
 def write_out(*refs):
@@ -321,6 +409,11 @@
             dma((steps,)), dma((steps,)), dma((steps,)), dma((steps,)),
             dma((3,)), dma((3,)), dma((2,)), dma((2,)),
             dma((8,)),
+            pltpu.VMEM((chunk, width), BF16),
+            pltpu.VMEM((chunk, width), BF16),
+            dma((2,)),
+            dma((2,)),
+            pltpu.SemaphoreType.REGULAR,
         ],
         compiler_params=pltpu.CompilerParams(
             collective_id=0, has_side_effects=True, vmem_limit_bytes=56 * 1024 * 1024

time: 51.7 us -> 49.1 us (0.950)
  Pallas kernels: 51 us -> 48.3 us
    pallas_call x1, Pallas kernels: 49.5 us -> 46.9 us  [body(): pl.pallas_call(lambda *refs: kernel(chunk, *refs), name='distill', out_sh...]
where the time goes in v4:
time: 49.1 us; the launch traced here: 49 us
  Pallas kernels  48.3 us (98%)
  between operations  0.64 us (1%)
    pallas_call x1, Pallas kernels, body(): pl.pallas_call(lambda *refs: kernel(chunk, *refs), name='distill', out_sh...  46.9 us
    pallas_call x1, Pallas kernels, body(): pl.pallas_call(write_out, name='write_out', out_shape=(jax.ShapeDtypeStru...  1.43 us

profile of v4, /device:TPU:1, one launch (start us, length us, event | category | flops | bytes accessed | tf_op | source)
XLA Modules:
  0.0 49.0 jit_solution(4973362905481824734)
XLA Ops:
  0.6 46.9 %distill.1 = (f32[6,128]{1,0:T(8,128)S(1)}, bf16[768,768]{1,0:T(8,128)(2,1)S(1)}, bf16[768,768]{1,0:T(8,128)(2,1)S(1)}) custom-call(bf16[768,768]{1,0:T(8,128)(2,1)} %refs_0_.1, bf16[768,768]{1,0:T(8,128)(2,1)} %refs_1_.1, bf16[768,768]{1,0:T(8,128)(2,1)} %refs_2_.1, f32[24,768]{1,0:T(8,128)} %bitcast.4, s32[6,128]{1,0:T(8,128)} %bitcast.5, ...), custom_call_target="tpu_custom_call" | custom-call | flops 13589544960 | bytes 7077888 | tf_op jit(solution)/shard_map/distill/pallas_call | solution.py:370
  47.6 1.4 %write_out.1 = (f32[6,128]{1,0:T(8,128)}, bf16[768,768]{1,0:T(8,128)(2,1)}, bf16[768,768]{1,0:T(8,128)(2,1)}) custom-call(f32[6,128]{1,0:T(8,128)S(1)} %get-tuple-element.9.refs_0_, bf16[768,768]{1,0:T(8,128)(2,1)S(1)} %get-tuple-element.10.refs_1_, bf16[768,768]{1,0:T(8,128)(2,1)S(1)} %get-tuple-element.11.refs_2_), custom_call_target="tpu_custom_call" | custom-call | tf_op jit(solution)/shard_map/write_out/pallas_call | solution.py:434

commit v5 on v4

--- a/solution.py
+++ b/solution.py
@@ -14,8 +14,8 @@
 TILE = 256
 CHUNK = 96
 GRID = (4, 8, 4)
-X_RELAYED, X_FORWARD = 4, 3
-G_RELAYED, G_FORWARD = 4, 7
+X_RELAYED, X_FORWARD = 5, 3
+G_RELAYED, G_FORWARD = 4, 6
 
 
 def dot(a, b, ca, cb):
@@ -108,7 +108,7 @@
     def greet(partner):
         pl.semaphore_signal(barrier, inc=1, device_id=(partner,), device_id_type=MESH)
 
-    for partner in (other, behind, ahead):
+    for partner in (ahead, behind, other):
         greet(partner)
 
     @pl.when(is_source)

time: 49.1 us -> 49.3 us (level)
  no operation moved by 1% of the time
where the time goes in v5:
time: 49.3 us; the launch traced here: 49 us
  Pallas kernels  48.4 us (98%)
  between operations  0.64 us (1%)
    pallas_call x1, Pallas kernels, body(): pl.pallas_call(lambda *refs: kernel(chunk, *refs), name='distill', out_sh...  47 us
    pallas_call x1, Pallas kernels, body(): pl.pallas_call(write_out, name='write_out', out_shape=(jax.ShapeDtypeStru...  1.43 us

profile of v5, /device:TPU:1, one launch (start us, length us, event | category | flops | bytes accessed | tf_op | source)
XLA Modules:
  0.0 49.0 jit_solution(2150029577797504138)
XLA Ops:
  0.6 47.0 %distill.1 = (f32[6,128]{1,0:T(8,128)S(1)}, bf16[768,768]{1,0:T(8,128)(2,1)S(1)}, bf16[768,768]{1,0:T(8,128)(2,1)S(1)}) custom-call(bf16[768,768]{1,0:T(8,128)(2,1)} %refs_0_.1, bf16[768,768]{1,0:T(8,128)(2,1)} %refs_1_.1, bf16[768,768]{1,0:T(8,128)(2,1)} %refs_2_.1, f32[24,768]{1,0:T(8,128)} %bitcast.4, s32[6,128]{1,0:T(8,128)} %bitcast.5, ...), custom_call_target="tpu_custom_call" | custom-call | flops 13589544960 | bytes 7077888 | tf_op jit(solution)/shard_map/distill/pallas_call | solution.py:370
  47.6 1.4 %write_out.1 = (f32[6,128]{1,0:T(8,128)}, bf16[768,768]{1,0:T(8,128)(2,1)}, bf16[768,768]{1,0:T(8,128)(2,1)}) custom-call(f32[6,128]{1,0:T(8,128)S(1)} %get-tuple-element.9.refs_0_, bf16[768,768]{1,0:T(8,128)(2,1)S(1)} %get-tuple-element.10.refs_1_, bf16[768,768]{1,0:T(8,128)(2,1)S(1)} %get-tuple-element.11.refs_2_), custom_call_target="tpu_custom_call" | custom-call | tf_op jit(solution)/shard_map/write_out/pallas_call | solution.py:434
